TPU v7x, 32 devices: a whole 2x2x4 slice. The times are simulated.
32 devices in a mesh: groups: 2 (over y), users: 4 (over z), hours: 4 (over x, core).
Axes of the slice: x: 2, y: 2, z: 4, core: 2. Of those that a mesh axis runs over, the one named last changes fastest.
Arguments:
- activity: bfloat16 [16384, 8192], P(('groups', 'users'), 'hours'), parts along dimension 0, may hold values from -6 to 6
- cohort: int32 [16384], P(('groups', 'users')), parts along dimension 0, may hold values from 0 to 15
- tap_table: float32 [16, 9], replicated, may hold values from 0.02 to 0.4
- sketch: bfloat16 [8192, 64], P('hours'), may hold values from -0.0625 to 0.0625
Outputs:
- basis: float32 [16384, 64], P(('groups', 'users', 'hours')), parts along dimension 0
- triangle: float32 [128, 64], P('groups'), parts along dimension 0
There are 2 independent parts, one for each index of `groups`. A program takes and returns all parts, laid end to end along the dimension named above; an argument that names none is the same for every part. Nothing has to cross between parts.
All inputs are finite; a program needn't handle non-finite values.
Results may differ from a plain program's by a relative error of at most 0.003.
Values may be sent and summed in bfloat16 or wider, within the bound.
A program may use at most 64 MiB of HBM per device.

v0:
```python
import functools
import math

import jax
import jax.numpy as jnp
from jax import lax
from jax.experimental import pallas as pl
from jax.experimental.pallas import tpu as pltpu
from jax.sharding import PartitionSpec as P

TAPS = 9
REACH = (TAPS - 1) // 2
EDGE = 128
PANEL = 8
HIGHEST = lax.Precision.HIGHEST
MESH = pl.DeviceIdType.MESH


def flip(index, mask):
    bit = 1
    while bit <= mask:
        if mask & bit:
            index = index + bit - 2 * bit * ((index // bit) % 2)
        bit *= 2
    return index


def dot_nt(a, b, precision=None):
    return lax.dot_general(
        a, b, (((1,), (1,)), ((), ())), precision=precision, preferred_element_type=jnp.float32
    )


def multiply(shifted, block, slot):
    share = block.shape[1]
    half = share // 2
    return jnp.concatenate(
        [dot_nt(shifted[...], block[slot, pl.ds(first, half), :]) for first in (0, half)], axis=1
    )


def eliminate(gram):
    k = gram.shape[0]
    row_id = lax.broadcasted_iota(jnp.int32, (k, 2 * k), 0)
    lane_id = lax.broadcasted_iota(jnp.int32, (k, 2 * k), 1)
    eye = (row_id[:, :k] == lane_id[:, :k]).astype(jnp.float32)
    work = jnp.concatenate([gram, eye], axis=1)
    diag_id = lax.broadcasted_iota(jnp.int32, (PANEL, 2 * k), 0)
    done = []
    for first in range(0, k, PANEL):
        rows = work.shape[0]
        below = lax.broadcasted_iota(jnp.int32, (rows, 2 * k), 0)
        cols = [
            jnp.broadcast_to(work[:, first + i : first + i + 1], (rows, 2 * k))
            for i in range(PANEL)
        ]
        pivots = jnp.zeros((PANEL, 2 * k), jnp.float32)
        for i in range(PANEL):
            pivot = cols[i][i : i + 1, :]
            pivots = jnp.where(diag_id == i, pivot, pivots)
            col = jnp.where(below > i, cols[i], 0.0) * (1.0 / pivot)
            for later in range(i + 1, PANEL):
                cols[later] = cols[later] - col * cols[i][later : later + 1, :]
            work = work - col * work[i : i + 1, :]
        done.append(work[:PANEL] * lax.rsqrt(pivots))
        work = work[PANEL:]
    work = jnp.concatenate(done, axis=0)
    upper = jnp.where(row_id[:, :k] <= lane_id[:, :k], work[:, :k], 0.0)
    inverse = jnp.where(row_id[:, :k] >= lane_id[:, :k], work[:, k:], 0.0)
    return upper, inverse


def pack(square):
    half = square.shape[0] // 2
    return jnp.concatenate([square[:half], square[half:]], axis=1)


def unpack(packed):
    k = packed.shape[1] // 2
    return jnp.concatenate([packed[:, :k], packed[:, k:]], axis=0)


def kernel(
    n_users, n_hours, activity, cohort, table, sketch, local_out, gram_out,
    block, edge, shifted, ends, taps, send, recv, send_far, recv_far, gram_h, gram_u,
    load_sem, edge_send, edge_recv, part_send, part_recv, gh_send, gh_recv, gu_send, gu_recv,
):
    users = lax.axis_index("users")
    hours = lax.axis_index("hours")
    rows, width = activity.shape
    k = sketch.shape[0]
    share = rows // n_hours

    order = list(range(n_hours - 1, 0, -1)) + [0]
    loads = []
    for mask in order:
        start = pl.multiple_of(flip(hours, mask) * share, share)
        load = pltpu.make_async_copy(
            activity.at[pl.ds(start, share), :], block.at[mask], load_sem.at[mask]
        )
        load.start()
        loads.append(load)

    barrier = pltpu.get_barrier_semaphore()
    for mask in range(1, n_hours):
        pl.semaphore_signal(
            barrier, inc=1, device_id={"hours": flip(hours, mask)}, device_id_type=MESH
        )
    for step in range(1, n_users):
        pl.semaphore_signal(
            barrier, inc=1, device_id={"users": (users + step) % n_users}, device_id_type=MESH
        )
    cohorts = table.shape[0]
    onehot = (
        lax.broadcasted_iota(jnp.int32, (cohorts, rows), 0) == cohort[...]
    ).astype(jnp.float32)
    taps[...] = lax.dot_general(
        table[...], onehot, (((0,), (0,)), ((), ())),
        precision=HIGHEST, preferred_element_type=jnp.float32,
    )

    middle = sketch[...].astype(jnp.float32)
    blank = jnp.zeros((k, EDGE), jnp.float32)
    turned = jnp.concatenate([blank, middle, blank], axis=1)
    for step in range(TAPS):
        shift = (step - REACH) % turned.shape[1]
        moved = turned if shift == 0 else pltpu.roll(turned, shift, 1)
        shifted[pl.ds(step * k, k), :] = moved[:, EDGE : EDGE + width].astype(jnp.bfloat16)

    pl.semaphore_wait(barrier, n_hours - 1 + n_users - 1)

    to_right = pltpu.make_async_remote_copy(
        src_ref=sketch.at[:, pl.ds(width - EDGE, EDGE)],
        dst_ref=edge.at[0],
        send_sem=edge_send.at[0],
        recv_sem=edge_recv.at[0],
        device_id={"hours": (hours + 1) % n_hours},
        device_id_type=MESH,
    )
    to_left = pltpu.make_async_remote_copy(
        src_ref=sketch.at[:, pl.ds(0, EDGE)],
        dst_ref=edge.at[1],
        send_sem=edge_send.at[1],
        recv_sem=edge_recv.at[1],
        device_id={"hours": (hours + n_hours - 1) % n_hours},
        device_id_type=MESH,
    )
    to_right.start()
    to_left.start()

    loads[0].wait()
    product = multiply(shifted, block, order[0])

    to_right.wait()
    to_left.wait()
    low = jnp.where(hours > 0, edge[0].astype(jnp.float32), blank)
    high = jnp.where(hours < n_hours - 1, edge[1].astype(jnp.float32), blank)
    turned = jnp.concatenate([low, blank, blank, high], axis=1)
    for step in range(TAPS):
        shift = (step - REACH) % turned.shape[1]
        moved = turned if shift == 0 else pltpu.roll(turned, shift, 1)
        ends[pl.ds(step * k, k), :] = moved[:, EDGE : 3 * EDGE].astype(jnp.bfloat16)
    shifted[:, pl.ds(0, EDGE)] += ends[:, pl.ds(0, EDGE)]
    shifted[:, pl.ds(width - EDGE, EDGE)] += ends[:, pl.ds(EDGE, EDGE)]
    outer = jnp.concatenate(
        [block[order[0], :, pl.ds(0, EDGE)], block[order[0], :, pl.ds(width - EDGE, EDGE)]], axis=1
    )
    product += dot_nt(ends[...], outer)

    copies = {}
    for load, mask in zip(loads, order):
        start = pl.multiple_of(flip(hours, mask) * share, share)
        if mask != order[0]:
            load.wait()
            product = multiply(shifted, block, mask)
        total = taps[pl.ds(0, 1), pl.ds(start, share)] * product[:k]
        for step in range(1, TAPS):
            total += (
                taps[pl.ds(step, 1), pl.ds(start, share)] * product[step * k : (step + 1) * k]
            )
        bit = 1
        while mask + bit < n_hours and (mask == 0 or bit < mask & -mask):
            copies[mask + bit].wait()
            arrived = recv if bit == 1 else recv_far
            total += arrived[mask + bit - 1].astype(jnp.float32)
            bit *= 2
        if mask:
            near = mask % 2 == 1
            source, target = (send, recv) if near else (send_far, recv_far)
            source[mask - 1] = total.astype(source.dtype)
            copies[mask] = pltpu.make_async_remote_copy(
                src_ref=source.at[mask - 1],
                dst_ref=target.at[mask - 1],
                send_sem=part_send.at[mask - 1],
                recv_sem=part_recv.at[mask - 1],
                device_id={"hours": flip(hours, mask & -mask)},
                device_id_type=MESH,
            )
            copies[mask].start()
    local = total
    local_out[...] = local

    gram = pack(dot_nt(local, local, HIGHEST))
    for axis, count, me, slots, send_sems, recv_sems in (
        ("hours", n_hours, hours, gram_h, gh_send, gh_recv),
        ("users", n_users, users, gram_u, gu_send, gu_recv),
    ):
        slots[me] = gram
        copies = []
        for step in range(1, count):
            copy = pltpu.make_async_remote_copy(
                src_ref=slots.at[me],
                dst_ref=slots.at[me],
                send_sem=send_sems.at[step - 1],
                recv_sem=recv_sems.at[step - 1],
                device_id={axis: (me + step) % count},
                device_id_type=MESH,
            )
            copy.start()
            copies.append(copy)
        for copy in copies:
            copy.wait()
        gram = slots[0]
        for slot in range(1, count):
            gram = gram + slots[slot]

    gram_out[...] = gram


def finish(scale, local, gram, basis, triangle):
    upper, inverse = eliminate(unpack(gram[...]))
    triangle[...] = upper * scale
    high = inverse.astype(jnp.bfloat16)
    rest = (inverse - high.astype(jnp.float32)).astype(jnp.bfloat16)
    values = local[...]
    main = values.astype(jnp.bfloat16)
    minor = (values - main.astype(jnp.float32)).astype(jnp.bfloat16)
    basis[...] = jnp.dot(
        jnp.concatenate([high, rest, high], axis=1),
        jnp.concatenate([main, main, minor], axis=0),
        preferred_element_type=jnp.float32,
    )


def per_device(activity, cohort, tap_table, sketch):
    n_users, n_hours = lax.axis_size("users"), lax.axis_size("hours")
    rows, width = activity.shape
    k = sketch.shape[1]
    share = rows // n_hours
    dma = lambda count: pltpu.SemaphoreType.DMA((count,))
    vmem = pl.BlockSpec(memory_space=pltpu.VMEM)
    local, gram = pl.pallas_call(
        functools.partial(kernel, n_users, n_hours),
        out_shape=(
            jax.ShapeDtypeStruct((k, share), jnp.float32),
            jax.ShapeDtypeStruct((k // 2, 2 * k), jnp.float32),
        ),
        in_specs=[pl.BlockSpec(memory_space=pl.ANY), vmem, vmem, vmem],
        out_specs=(vmem, vmem),
        scratch_shapes=[
            pltpu.VMEM((n_hours, share, width), jnp.bfloat16),
            pltpu.VMEM((2, k, EDGE), jnp.bfloat16),
            pltpu.VMEM((TAPS * k, width), jnp.bfloat16),
            pltpu.VMEM((TAPS * k, 2 * EDGE), jnp.bfloat16),
            pltpu.VMEM((TAPS, rows), jnp.float32),
            pltpu.VMEM((n_hours - 1, k, share), jnp.float32),
            pltpu.VMEM((n_hours - 1, k, share), jnp.float32),
            pltpu.VMEM((n_hours - 1, k, share), jnp.bfloat16),
            pltpu.VMEM((n_hours - 1, k, share), jnp.bfloat16),
            pltpu.VMEM((n_hours, k // 2, 2 * k), jnp.float32),
            pltpu.VMEM((n_users, k // 2, 2 * k), jnp.float32),
            dma(n_hours), dma(2), dma(2),
            dma(n_hours - 1), dma(n_hours - 1),
            dma(n_hours - 1), dma(n_hours - 1),
            dma(n_users - 1), dma(n_users - 1),
        ],
        compiler_params=pltpu.CompilerParams(
            collective_id=0, has_side_effects=True, vmem_limit_bytes=56 * 1024 * 1024
        ),
        name="range_finder",
    )(activity, cohort[None, :], tap_table, sketch.T)
    basis, triangle = pl.pallas_call(
        functools.partial(finish, 1.0 / math.sqrt(rows * n_users)),
        out_shape=(
            jax.ShapeDtypeStruct((k, share), jnp.float32),
            jax.ShapeDtypeStruct((k, k), jnp.float32),
        ),
        in_specs=[vmem, vmem],
        out_specs=(vmem, vmem),
        name="factor",
    )(local, gram)
    return basis.T, triangle


def solution(mesh):
    return jax.shard_map(
        per_device,
        mesh=mesh,
        in_specs=(P(("groups", "users"), "hours"), P(("groups", "users")), P(), P("hours", None)),
        out_specs=(P(("groups", "users", "hours"), None), P("groups", None)),
        check_vma=False,
    )
```

profile of v0, /device:TPU:0, one launch (start us, length us, event | category | flops | bytes accessed | tf_op | source)
XLA Modules:
  0.0 25.2 jit_solution(10738930272815901066)
XLA Ops:
  0.6 21.0 %range_finder.1 = (f32[64,512]{1,0:T(8,128)}, f32[32,128]{1,0:T(8,128)}) custom-call(bf16[2048,2048]{1,0:T(8,128)(2,1)} %activity.1, s32[1,2048]{1,0:T(1,128)} %bitcast.4, f32[16,9]{1,0:T(8,128)} %table.1, bf16[64,2048]{1,0:T(8,128)(2,1)} %bitcast.3), custom_call_target="tpu_custom_call" | custom-call | tf_op jit(solution)/shard_map/range_finder/pallas_call | solution.py:252
  21.6 3.6 %factor.1 = (f32[64,512]{1,0:T(8,128)}, f32[64,64]{1,0:T(8,128)}) custom-call(f32[64,512]{1,0:T(8,128)} %get-tuple-element.6.local, f32[32,128]{1,0:T(8,128)} %get-tuple-element.7.gram), custom_call_target="tpu_custom_call" | custom-call | tf_op jit(solution)/shard_map/factor/pallas_call | solution.py:282
where the time goes:
time: 25.3 us; the launch traced here: 25.2 us
  Pallas kernels  24.5 us (97%)
  between operations  0.64 us (3%)
    pallas_call x1, Pallas kernels, per_device(): pl.pallas_call(functools.partial(kernel, n_users, n_hours), out_shape=(ja...  21 us
    pallas_call x1, Pallas kernels, per_device(): pl.pallas_call(functools.partial(finish, 1.0 / math.sqrt(rows * n_users))...  3.57 us

commit v1 on v0

v1 whole, which is shorter than its diff:
```python
import functools
import math

import jax
import jax.numpy as jnp
from jax import lax
from jax.experimental import pallas as pl
from jax.experimental.pallas import tpu as pltpu
from jax.sharding import PartitionSpec as P

TAPS = 9
REACH = (TAPS - 1) // 2
EDGE = 128
SEAM = 2 * REACH
PICK = 16
PANEL = 8
HIGHEST = lax.Precision.HIGHEST
MESH = pl.DeviceIdType.MESH


def flip(index, mask):
    bit = 1
    while bit <= mask:
        if mask & bit:
            index = index + bit - 2 * bit * ((index // bit) % 2)
        bit *= 2
    return index


def dot_nt(a, b, precision=None):
    return lax.dot_general(
        a, b, (((1,), (1,)), ((), ())), precision=precision, preferred_element_type=jnp.float32
    )


def eliminate(gram):
    k = gram.shape[0]
    row_id = lax.broadcasted_iota(jnp.int32, (k, 2 * k), 0)
    lane_id = lax.broadcasted_iota(jnp.int32, (k, 2 * k), 1)
    eye = (row_id[:, :k] == lane_id[:, :k]).astype(jnp.float32)
    work = jnp.concatenate([gram, eye], axis=1)
    diag_id = lax.broadcasted_iota(jnp.int32, (PANEL, 2 * k), 0)
    done = []
    for first in range(0, k, PANEL):
        rows = work.shape[0]
        below = lax.broadcasted_iota(jnp.int32, (rows, 2 * k), 0)
        cols = [
            jnp.broadcast_to(work[:, first + i : first + i + 1], (rows, 2 * k))
            for i in range(PANEL)
        ]
        pivots = jnp.zeros((PANEL, 2 * k), jnp.float32)
        for i in range(PANEL):
            pivot = cols[i][i : i + 1, :]
            pivots = jnp.where(diag_id == i, pivot, pivots)
            col = jnp.where(below > i, cols[i], 0.0) * (1.0 / pivot)
            for later in range(i + 1, PANEL):
                cols[later] = cols[later] - col * cols[i][later : later + 1, :]
            work = work - col * work[i : i + 1, :]
        done.append(work[:PANEL] * lax.rsqrt(pivots))
        work = work[PANEL:]
    work = jnp.concatenate(done, axis=0)
    upper = jnp.where(row_id[:, :k] <= lane_id[:, :k], work[:, :k], 0.0)
    inverse = jnp.where(row_id[:, :k] >= lane_id[:, :k], work[:, k:], 0.0)
    return upper, inverse


def pack(square):
    half = square.shape[0] // 2
    return jnp.concatenate([square[:half], square[half:]], axis=1)


def unpack(packed):
    k = packed.shape[1] // 2
    return jnp.concatenate([packed[:, :k], packed[:, k:]], axis=0)


def combine(product, taps, k):
    total = taps[0:1, :] * product[:k]
    for step in range(1, TAPS):
        total += taps[step : step + 1, :] * product[step * k : (step + 1) * k]
    return total


def kernel(
    n_users, n_hours, activity, cohort_in, table_in, sketch_in, local_out, gram_out,
    block, cohort, table, sketch, shifted, taps, near_out, near_in, far_out, far_in,
    pick_out, picks, rims, gram_h, gram_u,
    load_sem, input_sem, near_send, near_recv, far_send, far_recv, pick_send, pick_recv,
    rim_send, rim_recv, gh_send, gh_recv, gu_send, gu_recv,
):
    users = lax.axis_index("users")
    hours = lax.axis_index("hours")
    rows, width = activity.shape
    k = sketch.shape[0]
    share = rows // n_hours
    half = share // 2

    order = list(range(n_hours - 1, 0, -1)) + [0]
    starts = [pl.multiple_of(flip(hours, mask) * share, share) for mask in range(n_hours)]
    inputs = [
        pltpu.make_async_copy(source, target, input_sem.at[i])
        for i, (source, target) in enumerate(
            ((sketch_in, sketch), (cohort_in, cohort), (table_in, table))
        )
    ]
    for copy in inputs:
        copy.start()
    loads = {}
    for mask in order:
        for part in range(2):
            load = pltpu.make_async_copy(
                activity.at[pl.ds(pl.multiple_of(starts[mask] + part * half, half), half), :],
                block.at[mask, pl.ds(part * half, half), :],
                load_sem.at[2 * mask + part],
            )
            load.start()
            loads[mask, part] = load

    barrier = pltpu.get_barrier_semaphore()
    for mask in range(1, n_hours):
        pl.semaphore_signal(
            barrier, inc=1, device_id={"hours": flip(hours, mask)}, device_id_type=MESH
        )
    for step in range(1, n_users):
        pl.semaphore_signal(
            barrier, inc=1, device_id={"users": (users + step) % n_users}, device_id_type=MESH
        )

    pick_row = lax.broadcasted_iota(jnp.int32, (PICK, width), 0)
    pick_lane = lax.broadcasted_iota(jnp.int32, (PICK, width), 1)
    wanted = jnp.where(pick_row < REACH, width - REACH + pick_row, pick_row - REACH)
    shifted[pl.ds(TAPS * k, PICK), :] = (
        (pick_lane == wanted) & (pick_row < SEAM)
    ).astype(jnp.bfloat16)

    inputs[0].wait()
    middle = sketch[...].astype(jnp.float32)
    lane = lax.broadcasted_iota(jnp.int32, (k, EDGE), 1)
    for step in range(TAPS):
        shift = step - REACH
        if shift == 0:
            shifted[pl.ds(step * k, k), :] = sketch[...]
            continue
        moved = pltpu.roll(middle, shift % width, 1)
        if shift > 0:
            first = jnp.where(lane < shift, 0.0, moved[:, :EDGE])
            moved = jnp.concatenate([first, moved[:, EDGE:]], axis=1)
        else:
            last = jnp.where(lane >= EDGE + shift, 0.0, moved[:, width - EDGE :])
            moved = jnp.concatenate([moved[:, : width - EDGE], last], axis=1)
        shifted[pl.ds(step * k, k), :] = moved.astype(jnp.bfloat16)

    inputs[1].wait()
    inputs[2].wait()
    cohorts = table.shape[0]
    onehot = (
        lax.broadcasted_iota(jnp.int32, (cohorts, rows), 0) == cohort[...]
    ).astype(jnp.float32)
    taps[...] = lax.dot_general(
        table[...], onehot, (((0,), (0,)), ((), ())),
        precision=HIGHEST, preferred_element_type=jnp.float32,
    )

    ends = jnp.where(
        lane < REACH,
        pltpu.roll(middle[:, width - EDGE :], REACH, 1),
        jnp.where(lane < SEAM, pltpu.roll(middle[:, :EDGE], REACH, 1), 0.0),
    )
    rims[hours] = ends

    waits = []

    def send(source, target, send_sem, recv_sem, mask):
        copy = pltpu.make_async_remote_copy(
            src_ref=source, dst_ref=target, send_sem=send_sem, recv_sem=recv_sem,
            device_id={"hours": flip(hours, mask)}, device_id_type=MESH,
        )
        copy.start()
        waits.append(copy)

    sums = {}
    for mask in order:
        for part in range(2):
            loads[mask, part].wait()
        product = jnp.concatenate(
            [
                dot_nt(shifted[...], block[mask, pl.ds(part * half, half), :])
                for part in range(2)
            ],
            axis=1,
        )
        total = combine(product, taps[:, pl.ds(starts[mask], share)], k)
        picked = product[TAPS * k : TAPS * k + SEAM]
        if mask == order[0]:
            pl.semaphore_wait(barrier, n_hours - 1 + n_users - 1)
            for other in range(1, n_hours):
                send(
                    rims.at[hours], rims.at[hours], rim_send.at[other - 1],
                    rim_recv.at[other - 1], other,
                )
        if mask == 0:
            picks[hours] = picked
            continue
        pick_out[mask - 1] = picked
        if mask == 1:
            near_out[...] = total
            send(near_out, near_in, near_send, near_recv, mask)
        else:
            far_out[mask - 2] = total.astype(jnp.bfloat16)
            send(
                far_out.at[mask - 2], far_in.at[mask - 2], far_send.at[mask - 2],
                far_recv.at[mask - 2], mask,
            )
        send(
            pick_out.at[mask - 1], picks.at[hours], pick_send.at[mask - 1],
            pick_recv.at[mask - 1], mask,
        )

    for copy in waits:
        copy.wait()

    seams = jnp.zeros((k, EDGE), jnp.float32)
    for index in range(n_hours - 1):
        left = jnp.where(lane < REACH, rims[index], 0.0)
        right = jnp.where(lane >= REACH, rims[index + 1], 0.0)
        both = left + right
        seams += both if index == 0 else pltpu.roll(both, SEAM * index, 1)
    row = lax.broadcasted_iota(jnp.int32, (SEAM, share), 0)
    beside = [
        jnp.where(row < REACH, picks[index], picks[index + 1]) for index in range(n_hours - 1)
    ]
    depth = EDGE // REACH
    beside = jnp.concatenate(
        beside + [jnp.zeros((depth - SEAM * (n_hours - 1), share), jnp.float32)], axis=0
    )
    place = lane % SEAM
    crossing, weighted = [], []
    for side in (-1, 1):
        panel = jnp.zeros((k, EDGE), jnp.float32)
        for index in range(REACH):
            shift = side * (index + 1)
            from_place = place - shift
            inside = (from_place >= 0) & (from_place < SEAM)
            across = (place < REACH) != (from_place < REACH)
            mine = (lane >= depth * index) & (lane < depth * (index + 1))
            moved = pltpu.roll(seams, (depth * index + shift) % EDGE, 1)
            panel = jnp.where(inside & across & mine, moved, panel)
            step = REACH + shift
            weighted.append(taps[pl.ds(step, 1), pl.ds(starts[0], share)] * beside)
        crossing.append(panel)
    total += jnp.dot(
        jnp.concatenate(crossing, axis=1).astype(jnp.bfloat16),
        jnp.concatenate(weighted, axis=0).astype(jnp.bfloat16),
        preferred_element_type=jnp.float32,
    )
    total += near_in[...]
    for mask in range(2, n_hours):
        total += far_in[mask - 2].astype(jnp.float32)
    local = total
    local_out[...] = local

    gram = pack(dot_nt(local, local, HIGHEST))
    for axis, count, me, slots, send_sems, recv_sems in (
        ("hours", n_hours, hours, gram_h, gh_send, gh_recv),
        ("users", n_users, users, gram_u, gu_send, gu_recv),
    ):
        slots[me] = gram
        copies = []
        for step in range(1, count):
            copy = pltpu.make_async_remote_copy(
                src_ref=slots.at[me],
                dst_ref=slots.at[me],
                send_sem=send_sems.at[step - 1],
                recv_sem=recv_sems.at[step - 1],
                device_id={axis: (me + step) % count},
                device_id_type=MESH,
            )
            copy.start()
            copies.append(copy)
        for copy in copies:
            copy.wait()
        gram = slots[0]
        for slot in range(1, count):
            gram = gram + slots[slot]

    gram_out[...] = gram


def finish(scale, local, gram, basis, triangle):
    upper, inverse = eliminate(unpack(gram[...]))
    triangle[...] = upper * scale
    high = inverse.astype(jnp.bfloat16)
    rest = (inverse - high.astype(jnp.float32)).astype(jnp.bfloat16)
    values = local[...]
    main = values.astype(jnp.bfloat16)
    minor = (values - main.astype(jnp.float32)).astype(jnp.bfloat16)
    basis[...] = jnp.dot(
        jnp.concatenate([high, rest, high], axis=1),
        jnp.concatenate([main, main, minor], axis=0),
        preferred_element_type=jnp.float32,
    )


def per_device(activity, cohort, tap_table, sketch):
    n_users, n_hours = lax.axis_size("users"), lax.axis_size("hours")
    rows, width = activity.shape
    k = sketch.shape[1]
    share = rows // n_hours
    dma = lambda count: pltpu.SemaphoreType.DMA((count,))
    one = pltpu.SemaphoreType.DMA
    vmem = pl.BlockSpec(memory_space=pltpu.VMEM)
    local, gram = pl.pallas_call(
        functools.partial(kernel, n_users, n_hours),
        out_shape=(
            pltpu.VMEM((k, share), jnp.float32),
            pltpu.VMEM((k // 2, 2 * k), jnp.float32),
        ),
        in_specs=[pl.BlockSpec(memory_space=pltpu.HBM)] * 4,
        out_specs=(vmem, vmem),
        scratch_shapes=[
            pltpu.VMEM((n_hours, share, width), jnp.bfloat16),
            pltpu.VMEM((1, rows), jnp.int32),
            pltpu.VMEM(tap_table.shape, jnp.float32),
            pltpu.VMEM((k, width), jnp.bfloat16),
            pltpu.VMEM((TAPS * k + PICK, width), jnp.bfloat16),
            pltpu.VMEM((TAPS, rows), jnp.float32),
            pltpu.VMEM((k, share), jnp.float32),
            pltpu.VMEM((k, share), jnp.float32),
            pltpu.VMEM((n_hours - 2, k, share), jnp.bfloat16),
            pltpu.VMEM((n_hours - 2, k, share), jnp.bfloat16),
            pltpu.VMEM((n_hours - 1, SEAM, share), jnp.float32),
            pltpu.VMEM((n_hours, SEAM, share), jnp.float32),
            pltpu.VMEM((n_hours, k, EDGE), jnp.float32),
            pltpu.VMEM((n_hours, k // 2, 2 * k), jnp.float32),
            pltpu.VMEM((n_users, k // 2, 2 * k), jnp.float32),
            dma(2 * n_hours), dma(3), one, one,
            dma(n_hours - 2), dma(n_hours - 2), dma(n_hours - 1), dma(n_hours - 1),
            dma(n_hours - 1), dma(n_hours - 1), dma(n_hours - 1), dma(n_hours - 1),
            dma(n_users - 1), dma(n_users - 1),
        ],
        compiler_params=pltpu.CompilerParams(
            collective_id=0, has_side_effects=True, vmem_limit_bytes=48 * 1024 * 1024
        ),
        name="range_finder",
    )(activity, cohort[None, :], tap_table, sketch.T)
    basis, triangle = pl.pallas_call(
        functools.partial(finish, 1.0 / math.sqrt(rows * n_users)),
        out_shape=(
            jax.ShapeDtypeStruct((k, share), jnp.float32),
            jax.ShapeDtypeStruct((k, k), jnp.float32),
        ),
        in_specs=[vmem, vmem],
        out_specs=(vmem, vmem),
        compiler_params=pltpu.CompilerParams(vmem_limit_bytes=8 * 1024 * 1024),
        name="factor",
    )(
        pltpu.with_memory_space_constraint(local, pltpu.VMEM),
        pltpu.with_memory_space_constraint(gram, pltpu.VMEM),
    )
    return basis.T, triangle


def solution(mesh):
    return jax.shard_map(
        per_device,
        mesh=mesh,
        in_specs=(P(("groups", "users"), "hours"), P(("groups", "users")), P(), P("hours", None)),
        out_specs=(P(("groups", "users", "hours"), None), P("groups", None)),
        check_vma=False,
    )
```

time: 25.3 us -> 26.1 us (1.032)
  local copies, waits for them, and re-layouts: 0 us -> 2.34 us
  Pallas kernels: 24.5 us -> 22.9 us
    unnamed x0 -> x6, local copies, waits for them, and re-layouts: none -> 2.34 us
    pallas_call x1, Pallas kernels: 3.57 us -> 2.66 us  [per_device(): pl.pallas_call(functools.partial(finish, 1.0 / math.sqrt(rows * n_users))...]
    pallas_call x1, Pallas kernels: 21 us -> 20.2 us  [per_device(): pl.pallas_call(functools.partial(kernel, n_users, n_hours), out_shape=(pl...]
where the time goes in v1:
time: 26.1 us; the launch traced here: 25.9 us
  Pallas kernels  22.9 us (88%)
  local copies, waits for them, and re-layouts  2.34 us (9%)
  between operations  0.65 us (2%)
    pallas_call x1, Pallas kernels, per_device(): pl.pallas_call(functools.partial(kernel, n_users, n_hours), out_shape=(pl...  20.2 us
    pallas_call x1, Pallas kernels, per_device(): pl.pallas_call(functools.partial(finish, 1.0 / math.sqrt(rows * n_users))...  2.66 us
    unnamed x6, local copies, waits for them, and re-layouts  2.34 us

profile of v1, /device:TPU:0, one launch (start us, length us, event | category | flops | bytes accessed | tf_op | source)
XLA Modules:
  0.0 25.9 jit_solution(14176515260554877046)
XLA Ops:
  0.6 0.0 copy-start
  0.6 0.9 %copy-done = bf16[2048,64]{0,1:T(8,128)(2,1)S(1)} copy-done((bf16[2048,64]{0,1:T(8,128)(2,1)S(1)}, bf16[2048,64]{0,1:T(8,128)(2,1)}, u32[]{:S(2)}) %copy-start) | copy-done | bytes 262168
  1.6 0.0 copy-start.1
  1.6 0.7 %copy-done.1 = s32[2048]{0:T(1024)S(1)} copy-done((s32[2048]{0:T(1024)S(1)}, s32[2048]{0:T(1024)}, u32[]{:S(2)}) %copy-start.1) | copy-done | bytes 8216
  2.3 0.0 copy-start.2
  2.3 0.7 %copy-done.2 = f32[16,9]{1,0:T(8,128)S(1)} copy-done((f32[16,9]{1,0:T(8,128)S(1)}, f32[16,9]{1,0:T(8,128)}, u32[]{:S(2)}) %copy-start.2) | copy-done | bytes 600
  3.0 20.2 %range_finder.1 = (f32[64,512]{1,0:T(8,128)S(1)}, f32[32,128]{1,0:T(8,128)S(1)}) custom-call(bf16[2048,2048]{1,0:T(8,128)(2,1)} %activity.1, s32[1,2048]{1,0:T(1,128)S(1)} %bitcast.4, f32[16,9]{1,0:T(8,128)S(1)} %copy-done.2, bf16[64,2048]{1,0:T(8,128)(2,1)S(1)} %bitcast.3), custom_call_target="tpu_custom_call" | custom-call | tf_op jit(solution)/shard_map/range_finder/pallas_call | solution.py:312
  23.2 2.7 %factor.1 = (f32[64,512]{1,0:T(8,128)}, f32[64,64]{1,0:T(8,128)}) custom-call(f32[64,512]{1,0:T(8,128)S(1)} %get-tuple-element.6.local, f32[32,128]{1,0:T(8,128)S(1)} %get-tuple-element.7.gram), custom_call_target="tpu_custom_call" | custom-call | tf_op jit(solution)/shard_map/factor/pallas_call | solution.py:346
Async XLA Ops:
  0.6 1.0 %copy-start = (bf16[2048,64]{0,1:T(8,128)(2,1)S(1)}, bf16[2048,64]{0,1:T(8,128)(2,1)}, u32[]{:S(2)}) copy-start(bf16[2048,64]{0,1:T(8,128)(2,1)} %param.7) | copy-start | bytes 786436
  1.6 0.7 %copy-start.1 = (s32[2048]{0:T(1024)S(1)}, s32[2048]{0:T(1024)}, u32[]{:S(2)}) copy-start(s32[2048]{0:T(1024)} %param.5) | copy-start | bytes 24580
  2.3 0.7 %copy-start.2 = (f32[16,9]{1,0:T(8,128)S(1)}, f32[16,9]{1,0:T(8,128)}, u32[]{:S(2)}) copy-start(f32[16,9]{1,0:T(8,128)} %table_in.1) | copy-start | bytes 1732

commit v2 on v1

--- a/solution.py
+++ b/solution.py
@@ -100,7 +100,7 @@
     inputs = [
         pltpu.make_async_copy(source, target, input_sem.at[i])
         for i, (source, target) in enumerate(
-            ((sketch_in, sketch), (cohort_in, cohort), (table_in, table))
+            ((cohort_in, cohort), (table_in, table), (sketch_in, sketch))
         )
     ]
     for copy in inputs:
@@ -113,8 +113,14 @@
                 block.at[mask, pl.ds(part * half, half), :],
                 load_sem.at[2 * mask + part],
             )
-            load.start()
             loads[mask, part] = load
+
+    def fetch(index):
+        if index < n_hours:
+            for part in range(2):
+                loads[order[index], part].start()
+
+    fetch(0)
 
     barrier = pltpu.get_barrier_semaphore()
     for mask in range(1, n_hours):
@@ -134,6 +140,18 @@
     ).astype(jnp.bfloat16)
 
     inputs[0].wait()
+    inputs[1].wait()
+    cohorts = table.shape[0]
+    onehot = (
+        lax.broadcasted_iota(jnp.int32, (cohorts, rows), 0) == cohort[...]
+    ).astype(jnp.float32)
+    taps[...] = lax.dot_general(
+        table[...], onehot, (((0,), (0,)), ((), ())),
+        precision=HIGHEST, preferred_element_type=jnp.float32,
+    )
+
+    inputs[2].wait()
+    fetch(1)
     middle = sketch[...].astype(jnp.float32)
     lane = lax.broadcasted_iota(jnp.int32, (k, EDGE), 1)
     for step in range(TAPS):
@@ -150,17 +168,6 @@
             moved = jnp.concatenate([moved[:, : width - EDGE], last], axis=1)
         shifted[pl.ds(step * k, k), :] = moved.astype(jnp.bfloat16)
 
-    inputs[1].wait()
-    inputs[2].wait()
-    cohorts = table.shape[0]
-    onehot = (
-        lax.broadcasted_iota(jnp.int32, (cohorts, rows), 0) == cohort[...]
-    ).astype(jnp.float32)
-    taps[...] = lax.dot_general(
-        table[...], onehot, (((0,), (0,)), ((), ())),
-        precision=HIGHEST, preferred_element_type=jnp.float32,
-    )
-
     ends = jnp.where(
         lane < REACH,
         pltpu.roll(middle[:, width - EDGE :], REACH, 1),
@@ -179,9 +186,10 @@
         waits.append(copy)
 
     sums = {}
-    for mask in order:
+    for index, mask in enumerate(order):
         for part in range(2):
             loads[mask, part].wait()
+        fetch(index + 2)
         product = jnp.concatenate(
             [
                 dot_nt(shifted[...], block[mask, pl.ds(part * half, half), :])
@@ -342,7 +350,10 @@
             collective_id=0, has_side_effects=True, vmem_limit_bytes=48 * 1024 * 1024
         ),
         name="range_finder",
-    )(activity, cohort[None, :], tap_table, sketch.T)
+    )(*(
+        pltpu.with_memory_space_constraint(array, pltpu.HBM)
+        for array in (activity, cohort[None, :], tap_table, sketch.T)
+    ))
     basis, triangle = pl.pallas_call(
         functools.partial(finish, 1.0 / math.sqrt(rows * n_users)),
         out_shape=(

time: 26.1 us -> 23.8 us (0.912)
  local copies, waits for them, and re-layouts: 2.34 us -> 0 us
    unnamed x6 -> x0, local copies, waits for them, and re-layouts: 2.34 us -> none
where the time goes in v2:
time: 23.8 us; the launch traced here: 23.6 us
  Pallas kernels  23 us (97%)
  between operations  0.64 us (3%)
    pallas_call x1, Pallas kernels, per_device(): pl.pallas_call(functools.partial(kernel, n_users, n_hours), out_shape=(pl...  20.3 us
    pallas_call x1, Pallas kernels, per_device(): pl.pallas_call(functools.partial(finish, 1.0 / math.sqrt(rows * n_users))...  2.66 us

profile of v2, /device:TPU:0, one launch (start us, length us, event | category | flops | bytes accessed | tf_op | source)
XLA Modules:
  0.0 23.6 jit_solution(12335194907288205376)
XLA Ops:
  0.6 20.3 %range_finder.1 = (f32[64,512]{1,0:T(8,128)S(1)}, f32[32,128]{1,0:T(8,128)S(1)}) custom-call(bf16[2048,2048]{1,0:T(8,128)(2,1)} %activity.1, s32[1,2048]{1,0:T(1,128)} %bitcast.4, f32[16,9]{1,0:T(8,128)} %table_in.1, bf16[64,2048]{1,0:T(8,128)(2,1)} %bitcast.3), custom_call_target="tpu_custom_call" | custom-call | tf_op jit(solution)/shard_map/range_finder/pallas_call | solution.py:320
  21.0 2.7 %factor.1 = (f32[64,512]{1,0:T(8,128)}, f32[64,64]{1,0:T(8,128)}) custom-call(f32[64,512]{1,0:T(8,128)S(1)} %get-tuple-element.6.local, f32[32,128]{1,0:T(8,128)S(1)} %get-tuple-element.7.gram), custom_call_target="tpu_custom_call" | custom-call | tf_op jit(solution)/shard_map/factor/pallas_call | solution.py:357

commit v3 on v2

--- a/solution.py
+++ b/solution.py
@@ -65,13 +65,37 @@
 
 
 def pack(square):
-    half = square.shape[0] // 2
-    return jnp.concatenate([square[:half], square[half:]], axis=1)
+    k = square.shape[0]
+    half = k // 2
+    row = lax.broadcasted_iota(jnp.int32, (half, half), 0)
+    col = lax.broadcasted_iota(jnp.int32, (half, half), 1)
+    corner = square[half:, half:]
+    folded = jnp.where(col >= row, square[:half, :half], corner)
+    wide = jnp.concatenate([folded, square[:half, half:]], axis=1)
+    diagonal = jnp.sum(jnp.where(row == col, corner, 0.0), axis=0, keepdims=True)
+    diagonal = jnp.concatenate([diagonal, jnp.zeros((1, 2 * k - half), jnp.float32)], axis=1)
+    quarter = half // 2
+    return jnp.concatenate([wide[:quarter], wide[quarter:]], axis=1), diagonal
 
 
 def unpack(packed):
     k = packed.shape[1] // 2
-    return jnp.concatenate([packed[:, :k], packed[:, k:]], axis=0)
+    half, quarter = k // 2, k // 4
+    row = lax.broadcasted_iota(jnp.int32, (half, half), 0)
+    col = lax.broadcasted_iota(jnp.int32, (half, half), 1)
+    wide = jnp.concatenate([packed[:quarter, :k], packed[:quarter, k:]], axis=0)
+    turned = wide.T
+    upper, lower = wide[:, :half], turned[:half]
+    corner = jnp.where(col < row, upper, lower)
+    corner = jnp.where(col == row, packed[quarter : quarter + 1, :half], corner)
+    first = jnp.where(col >= row, upper, lower)
+    return jnp.concatenate(
+        [
+            jnp.concatenate([first, wide[:, half:]], axis=1),
+            jnp.concatenate([turned[half:], corner], axis=1),
+        ],
+        axis=0,
+    )
 
 
 def combine(product, taps, k):
@@ -84,9 +108,9 @@
 def kernel(
     n_users, n_hours, activity, cohort_in, table_in, sketch_in, local_out, gram_out,
     block, cohort, table, sketch, shifted, taps, near_out, near_in, far_out, far_in,
-    pick_out, picks, rims, gram_h, gram_u,
+    pick_out, picks, rims, grams,
     load_sem, input_sem, near_send, near_recv, far_send, far_recv, pick_send, pick_recv,
-    rim_send, rim_recv, gh_send, gh_recv, gu_send, gu_recv,
+    rim_send, rim_recv, gram_send, gram_recv,
 ):
     users = lax.axis_index("users")
     hours = lax.axis_index("hours")
@@ -123,14 +147,14 @@
     fetch(0)
 
     barrier = pltpu.get_barrier_semaphore()
-    for mask in range(1, n_hours):
-        pl.semaphore_signal(
-            barrier, inc=1, device_id={"hours": flip(hours, mask)}, device_id_type=MESH
-        )
-    for step in range(1, n_users):
-        pl.semaphore_signal(
-            barrier, inc=1, device_id={"users": (users + step) % n_users}, device_id_type=MESH
-        )
+    peers = [
+        {"users": flip(users, far), "hours": flip(hours, mask)}
+        for far in range(n_users - 1, -1, -1)
+        for mask in range(n_hours - 1, -1, -1)
+        if far or mask
+    ]
+    for peer in peers:
+        pl.semaphore_signal(barrier, inc=1, device_id=peer, device_id_type=MESH)
 
     pick_row = lax.broadcasted_iota(jnp.int32, (PICK, width), 0)
     pick_lane = lax.broadcasted_iota(jnp.int32, (PICK, width), 1)
@@ -175,7 +199,7 @@
     )
     rims[hours] = ends
 
-    waits = []
+    small, late = [], []
 
     def send(source, target, send_sem, recv_sem, mask):
         copy = pltpu.make_async_remote_copy(
@@ -183,7 +207,7 @@
             device_id={"hours": flip(hours, mask)}, device_id_type=MESH,
         )
         copy.start()
-        waits.append(copy)
+        return copy
 
     sums = {}
     for index, mask in enumerate(order):
@@ -200,31 +224,31 @@
         total = combine(product, taps[:, pl.ds(starts[mask], share)], k)
         picked = product[TAPS * k : TAPS * k + SEAM]
         if mask == order[0]:
-            pl.semaphore_wait(barrier, n_hours - 1 + n_users - 1)
+            pl.semaphore_wait(barrier, len(peers))
             for other in range(1, n_hours):
-                send(
+                small.append(send(
                     rims.at[hours], rims.at[hours], rim_send.at[other - 1],
                     rim_recv.at[other - 1], other,
-                )
+                ))
         if mask == 0:
             picks[hours] = picked
             continue
         pick_out[mask - 1] = picked
+        small.append(send(
+            pick_out.at[mask - 1], picks.at[hours], pick_send.at[mask - 1],
+            pick_recv.at[mask - 1], mask,
+        ))
         if mask == 1:
             near_out[...] = total
-            send(near_out, near_in, near_send, near_recv, mask)
+            late.append(send(near_out, near_in, near_send, near_recv, mask))
         else:
             far_out[mask - 2] = total.astype(jnp.bfloat16)
-            send(
+            late.append(send(
                 far_out.at[mask - 2], far_in.at[mask - 2], far_send.at[mask - 2],
                 far_recv.at[mask - 2], mask,
-            )
-        send(
-            pick_out.at[mask - 1], picks.at[hours], pick_send.at[mask - 1],
-            pick_recv.at[mask - 1], mask,
-        )
-
-    for copy in waits:
+            ))
+
+    for copy in small:
         copy.wait()
 
     seams = jnp.zeros((k, EDGE), jnp.float32)
@@ -261,37 +285,38 @@
         jnp.concatenate(weighted, axis=0).astype(jnp.bfloat16),
         preferred_element_type=jnp.float32,
     )
+    for copy in reversed(late):
+        copy.wait()
     total += near_in[...]
     for mask in range(2, n_hours):
         total += far_in[mask - 2].astype(jnp.float32)
     local = total
     local_out[...] = local
 
-    gram = pack(dot_nt(local, local, HIGHEST))
-    for axis, count, me, slots, send_sems, recv_sems in (
-        ("hours", n_hours, hours, gram_h, gh_send, gh_recv),
-        ("users", n_users, users, gram_u, gu_send, gu_recv),
-    ):
-        slots[me] = gram
-        copies = []
-        for step in range(1, count):
-            copy = pltpu.make_async_remote_copy(
-                src_ref=slots.at[me],
-                dst_ref=slots.at[me],
-                send_sem=send_sems.at[step - 1],
-                recv_sem=recv_sems.at[step - 1],
-                device_id={axis: (me + step) % count},
-                device_id_type=MESH,
-            )
-            copy.start()
-            copies.append(copy)
-        for copy in copies:
-            copy.wait()
-        gram = slots[0]
-        for slot in range(1, count):
-            gram = gram + slots[slot]
-
+    me = users * n_hours + hours
+    folded, diagonal = pack(dot_nt(local, local, HIGHEST))
+    grams[me, pl.ds(0, k // 4), :] = folded
+    grams[me, pl.ds(k // 4, 1), :] = diagonal
+    copies = []
+    for index, peer in enumerate(peers):
+        copy = pltpu.make_async_remote_copy(
+            src_ref=grams.at[me],
+            dst_ref=grams.at[me],
+            send_sem=gram_send.at[index],
+            recv_sem=gram_recv.at[index],
+            device_id=peer,
+            device_id_type=MESH,
+        )
+        copy.start()
+        copies.append(copy)
+    for copy in copies:
+        copy.wait_recv()
+    gram = grams[0]
+    for slot in range(1, n_users * n_hours):
+        gram = gram + grams[slot]
     gram_out[...] = gram
+    for copy in copies:
+        copy.wait_send()
 
 
 def finish(scale, local, gram, basis, triangle):
@@ -321,7 +346,7 @@
         functools.partial(kernel, n_users, n_hours),
         out_shape=(
             pltpu.VMEM((k, share), jnp.float32),
-            pltpu.VMEM((k // 2, 2 * k), jnp.float32),
+            pltpu.VMEM((k // 4 + 1, 2 * k), jnp.float32),
         ),
         in_specs=[pl.BlockSpec(memory_space=pltpu.HBM)] * 4,
         out_specs=(vmem, vmem),
@@ -339,12 +364,11 @@
             pltpu.VMEM((n_hours - 1, SEAM, share), jnp.float32),
             pltpu.VMEM((n_hours, SEAM, share), jnp.float32),
             pltpu.VMEM((n_hours, k, EDGE), jnp.float32),
-            pltpu.VMEM((n_hours, k // 2, 2 * k), jnp.float32),
-            pltpu.VMEM((n_users, k // 2, 2 * k), jnp.float32),
+            pltpu.VMEM((n_users * n_hours, k // 4 + 1, 2 * k), jnp.float32),
             dma(2 * n_hours), dma(3), one, one,
             dma(n_hours - 2), dma(n_hours - 2), dma(n_hours - 1), dma(n_hours - 1),
-            dma(n_hours - 1), dma(n_hours - 1), dma(n_hours - 1), dma(n_hours - 1),
-            dma(n_users - 1), dma(n_users - 1),
+            dma(n_hours - 1), dma(n_hours - 1),
+            dma(n_users * n_hours - 1), dma(n_users * n_hours - 1),
         ],
         compiler_params=pltpu.CompilerParams(
             collective_id=0, has_side_effects=True, vmem_limit_bytes=48 * 1024 * 1024

time: 23.8 us -> 22.3 us (0.937)
  Pallas kernels: 23 us -> 21.5 us
    pallas_call x1, Pallas kernels: 20.3 us -> 18.8 us  [per_device(): pl.pallas_call(functools.partial(kernel, n_users, n_hours), out_shape=(pl...]
where the time goes in v3:
time: 22.3 us; the launch traced here: 22.1 us
  Pallas kernels  21.5 us (96%)
  between operations  0.64 us (3%)
    pallas_call x1, Pallas kernels, per_device(): pl.pallas_call(functools.partial(kernel, n_users, n_hours), out_shape=(pl...  18.8 us
    pallas_call x1, Pallas kernels, per_device(): pl.pallas_call(functools.partial(finish, 1.0 / math.sqrt(rows * n_users))...  2.73 us

profile of v3, /device:TPU:0, one launch (start us, length us, event | category | flops | bytes accessed | tf_op | source)
XLA Modules:
  0.0 22.1 jit_solution(13005984977449965019)
XLA Ops:
  0.6 18.8 %range_finder.1 = (f32[64,512]{1,0:T(8,128)S(1)}, f32[17,128]{1,0:T(8,128)S(1)}) custom-call(bf16[2048,2048]{1,0:T(8,128)(2,1)} %activity.1, s32[1,2048]{1,0:T(1,128)} %bitcast.4, f32[16,9]{1,0:T(8,128)} %table_in.1, bf16[64,2048]{1,0:T(8,128)(2,1)} %bitcast.3), custom_call_target="tpu_custom_call" | custom-call | tf_op jit(solution)/shard_map/range_finder/pallas_call | solution.py:345
  19.4 2.7 %factor.1 = (f32[64,512]{1,0:T(8,128)}, f32[64,64]{1,0:T(8,128)}) custom-call(f32[64,512]{1,0:T(8,128)S(1)} %get-tuple-element.6.local, f32[17,128]{1,0:T(8,128)S(1)} %get-tuple-element.7.gram), custom_call_target="tpu_custom_call" | custom-call | tf_op jit(solution)/shard_map/factor/pallas_call | solution.py:381

commit v4 on v3

--- a/solution.py
+++ b/solution.py
@@ -13,7 +13,7 @@
 EDGE = 128
 SEAM = 2 * REACH
 PICK = 16
-PANEL = 8
+PANEL = 16
 HIGHEST = lax.Precision.HIGHEST
 MESH = pl.DeviceIdType.MESH
 
@@ -39,7 +39,6 @@
     lane_id = lax.broadcasted_iota(jnp.int32, (k, 2 * k), 1)
     eye = (row_id[:, :k] == lane_id[:, :k]).astype(jnp.float32)
     work = jnp.concatenate([gram, eye], axis=1)
-    diag_id = lax.broadcasted_iota(jnp.int32, (PANEL, 2 * k), 0)
     done = []
     for first in range(0, k, PANEL):
         rows = work.shape[0]
@@ -48,15 +47,22 @@
             jnp.broadcast_to(work[:, first + i : first + i + 1], (rows, 2 * k))
             for i in range(PANEL)
         ]
-        pivots = jnp.zeros((PANEL, 2 * k), jnp.float32)
-        for i in range(PANEL):
-            pivot = cols[i][i : i + 1, :]
-            pivots = jnp.where(diag_id == i, pivot, pivots)
-            col = jnp.where(below > i, cols[i], 0.0) * (1.0 / pivot)
-            for later in range(i + 1, PANEL):
-                cols[later] = cols[later] - col * cols[i][later : later + 1, :]
-            work = work - col * work[i : i + 1, :]
-        done.append(work[:PANEL] * lax.rsqrt(pivots))
+        for i in range(0, PANEL, 2):
+            x, y = cols[i], cols[i + 1]
+            a, b, d = x[i : i + 1, :], x[i + 1 : i + 2, :], y[i + 1 : i + 2, :]
+            det = a * d - b * b
+            inverse_det = 1.0 / det
+            p = jnp.where(below > i + 1, d * x - b * y, 0.0) * inverse_det
+            q = jnp.where(below > i + 1, a * y - b * x, 0.0) * inverse_det
+            for later in range(i + 2, PANEL):
+                cols[later] = cols[later] - (
+                    p * x[later : later + 1, :] + q * y[later : later + 1, :]
+                )
+            top, second = work[i : i + 1, :], work[i + 1 : i + 2, :]
+            work = work - (p * top + q * second)
+            root = lax.rsqrt(a)
+            done.append(top * root)
+            done.append((second - (b * (1.0 / a)) * top) * (lax.rsqrt(det) * (a * root)))
         work = work[PANEL:]
     work = jnp.concatenate(done, axis=0)
     upper = jnp.where(row_id[:, :k] <= lane_id[:, :k], work[:, :k], 0.0)
@@ -64,14 +70,21 @@
     return upper, inverse
 
 
-def pack(square):
-    k = square.shape[0]
+def square(values):
+    main = values.astype(jnp.bfloat16)
+    minor = (values - main.astype(jnp.float32)).astype(jnp.bfloat16)
+    both = dot_nt(main, minor)
+    return dot_nt(main, main) + (both + both.T)
+
+
+def pack(gram):
+    k = gram.shape[0]
     half = k // 2
     row = lax.broadcasted_iota(jnp.int32, (half, half), 0)
     col = lax.broadcasted_iota(jnp.int32, (half, half), 1)
-    corner = square[half:, half:]
-    folded = jnp.where(col >= row, square[:half, :half], corner)
-    wide = jnp.concatenate([folded, square[:half, half:]], axis=1)
+    corner = gram[half:, half:]
+    folded = jnp.where(col >= row, gram[:half, :half], corner)
+    wide = jnp.concatenate([folded, gram[:half, half:]], axis=1)
     diagonal = jnp.sum(jnp.where(row == col, corner, 0.0), axis=0, keepdims=True)
     diagonal = jnp.concatenate([diagonal, jnp.zeros((1, 2 * k - half), jnp.float32)], axis=1)
     quarter = half // 2
@@ -109,7 +122,7 @@
     n_users, n_hours, activity, cohort_in, table_in, sketch_in, local_out, gram_out,
     block, cohort, table, sketch, shifted, taps, near_out, near_in, far_out, far_in,
     pick_out, picks, rims, grams,
-    load_sem, input_sem, near_send, near_recv, far_send, far_recv, pick_send, pick_recv,
+    row_ready, load_sem, input_sem, part_send, part_recv, pick_send, pick_recv,
     rim_send, rim_recv, gram_send, gram_recv,
 ):
     users = lax.axis_index("users")
@@ -153,7 +166,8 @@
         for mask in range(n_hours - 1, -1, -1)
         if far or mask
     ]
-    for peer in peers:
+    columns = [{"users": flip(users, far)} for far in range(n_users - 1, 0, -1)]
+    for peer in [{"hours": flip(hours, mask)} for mask in range(n_hours - 1, 0, -1)] + columns:
         pl.semaphore_signal(barrier, inc=1, device_id=peer, device_id_type=MESH)
 
     pick_row = lax.broadcasted_iota(jnp.int32, (PICK, width), 0)
@@ -165,6 +179,9 @@
 
     inputs[0].wait()
     inputs[1].wait()
+    inputs[2].wait()
+    fetch(1)
+    middle = sketch[...].astype(jnp.float32)
     cohorts = table.shape[0]
     onehot = (
         lax.broadcasted_iota(jnp.int32, (cohorts, rows), 0) == cohort[...]
@@ -174,32 +191,38 @@
         precision=HIGHEST, preferred_element_type=jnp.float32,
     )
 
-    inputs[2].wait()
-    fetch(1)
-    middle = sketch[...].astype(jnp.float32)
     lane = lax.broadcasted_iota(jnp.int32, (k, EDGE), 1)
-    for step in range(TAPS):
-        shift = step - REACH
-        if shift == 0:
-            shifted[pl.ds(step * k, k), :] = sketch[...]
-            continue
-        moved = pltpu.roll(middle, shift % width, 1)
-        if shift > 0:
-            first = jnp.where(lane < shift, 0.0, moved[:, :EDGE])
-            moved = jnp.concatenate([first, moved[:, EDGE:]], axis=1)
-        else:
-            last = jnp.where(lane >= EDGE + shift, 0.0, moved[:, width - EDGE :])
-            moved = jnp.concatenate([moved[:, : width - EDGE], last], axis=1)
-        shifted[pl.ds(step * k, k), :] = moved.astype(jnp.bfloat16)
+    blank = jnp.zeros((k, EDGE), jnp.float32)
+    padded = jnp.concatenate([blank, middle, blank], axis=1)
+    for part in range(2):
+        loads[order[0], part].wait()
+    piece = width // 4
+    products = [None, None]
+    for first in range(0, width, piece):
+        near_part = padded[:, first : first + piece + 2 * EDGE]
+        for step in range(TAPS):
+            shift = (step - REACH) % (piece + 2 * EDGE)
+            moved = near_part if shift == 0 else pltpu.roll(near_part, shift, 1)
+            shifted[pl.ds(step * k, k), pl.ds(first, piece)] = moved[
+                :, EDGE : EDGE + piece
+            ].astype(jnp.bfloat16)
+        for part in range(2):
+            partial = dot_nt(
+                shifted[:, pl.ds(first, piece)],
+                block[order[0], pl.ds(part * half, half), pl.ds(first, piece)],
+            )
+            products[part] = partial if first == 0 else products[part] + partial
 
     ends = jnp.where(
         lane < REACH,
         pltpu.roll(middle[:, width - EDGE :], REACH, 1),
         jnp.where(lane < SEAM, pltpu.roll(middle[:, :EDGE], REACH, 1), 0.0),
     )
-    rims[hours] = ends
-
-    small, late = [], []
+    rims[hours] = jnp.concatenate(
+        [ends.T[:SEAM], jnp.zeros((SEAM, EDGE - k), jnp.float32)], axis=1
+    )
+
+    small, copies = [], {}
 
     def send(source, target, send_sem, recv_sem, mask):
         copy = pltpu.make_async_remote_copy(
@@ -209,22 +232,26 @@
         copy.start()
         return copy
 
-    sums = {}
     for index, mask in enumerate(order):
+        if index:
+            for part in range(2):
+                loads[mask, part].wait()
+        fetch(index + 2)
+        sums, picked = [], []
         for part in range(2):
-            loads[mask, part].wait()
-        fetch(index + 2)
-        product = jnp.concatenate(
-            [
-                dot_nt(shifted[...], block[mask, pl.ds(part * half, half), :])
-                for part in range(2)
-            ],
-            axis=1,
-        )
-        total = combine(product, taps[:, pl.ds(starts[mask], share)], k)
-        picked = product[TAPS * k : TAPS * k + SEAM]
+            if index:
+                product = dot_nt(shifted[...], block[mask, pl.ds(part * half, half), :])
+            else:
+                product = products[part]
+            start = pl.multiple_of(starts[mask] + part * half, half)
+            sums.append(combine(product, taps[:, pl.ds(start, half)], k))
+            picked.append(product[TAPS * k : TAPS * k + SEAM])
+        total = jnp.concatenate(sums, axis=1)
+        picked = jnp.concatenate(picked, axis=0).astype(jnp.bfloat16)
         if mask == order[0]:
-            pl.semaphore_wait(barrier, len(peers))
+            pl.semaphore_wait(barrier, n_hours + n_users - 2)
+            for peer in columns:
+                pl.semaphore_signal(row_ready, inc=1, device_id=peer, device_id_type=MESH)
             for other in range(1, n_hours):
                 small.append(send(
                     rims.at[hours], rims.at[hours], rim_send.at[other - 1],
@@ -233,37 +260,47 @@
         if mask == 0:
             picks[hours] = picked
             continue
+        bit = 1
+        while mask + bit < n_hours and bit < mask & -mask:
+            copies[mask + bit].wait()
+            arrived = near_in if bit == 1 else far_in
+            total += arrived[mask + bit - 1].astype(jnp.float32)
+            bit *= 2
+        near = mask % 2 == 1
+        source, target = (near_out, near_in) if near else (far_out, far_in)
+        source[mask - 1] = total.astype(source.dtype)
+        copies[mask] = send(
+            source.at[mask - 1], target.at[mask - 1], part_send.at[mask - 1],
+            part_recv.at[mask - 1], mask & -mask,
+        )
         pick_out[mask - 1] = picked
         small.append(send(
             pick_out.at[mask - 1], picks.at[hours], pick_send.at[mask - 1],
             pick_recv.at[mask - 1], mask,
         ))
-        if mask == 1:
-            near_out[...] = total
-            late.append(send(near_out, near_in, near_send, near_recv, mask))
-        else:
-            far_out[mask - 2] = total.astype(jnp.bfloat16)
-            late.append(send(
-                far_out.at[mask - 2], far_in.at[mask - 2], far_send.at[mask - 2],
-                far_recv.at[mask - 2], mask,
-            ))
 
     for copy in small:
         copy.wait()
 
-    seams = jnp.zeros((k, EDGE), jnp.float32)
-    for index in range(n_hours - 1):
-        left = jnp.where(lane < REACH, rims[index], 0.0)
-        right = jnp.where(lane >= REACH, rims[index + 1], 0.0)
-        both = left + right
-        seams += both if index == 0 else pltpu.roll(both, SEAM * index, 1)
-    row = lax.broadcasted_iota(jnp.int32, (SEAM, share), 0)
-    beside = [
-        jnp.where(row < REACH, picks[index], picks[index + 1]) for index in range(n_hours - 1)
-    ]
     depth = EDGE // REACH
-    beside = jnp.concatenate(
-        beside + [jnp.zeros((depth - SEAM * (n_hours - 1), share), jnp.float32)], axis=0
+    rest = depth - SEAM * (n_hours - 1)
+
+    def beside_seams(slots, count):
+        row = lax.broadcasted_iota(jnp.int32, (SEAM, count), 0)
+        return jnp.concatenate(
+            [
+                jnp.where(row < REACH, slots[index], slots[index + 1])
+                for index in range(n_hours - 1)
+            ]
+            + [jnp.zeros((rest, count), jnp.float32)],
+            axis=0,
+        )
+
+    seams = beside_seams([rims[index] for index in range(n_hours)], EDGE).T[:k]
+    seams = jnp.concatenate([seams, jnp.zeros((k, EDGE - depth), jnp.float32)], axis=1)
+    flat = [picks[index].astype(jnp.float32) for index in range(n_hours)]
+    beside = beside_seams(
+        [jnp.concatenate([pick[:SEAM], pick[SEAM:]], axis=1) for pick in flat], share
     )
     place = lane % SEAM
     crossing, weighted = [], []
@@ -285,18 +322,20 @@
         jnp.concatenate(weighted, axis=0).astype(jnp.bfloat16),
         preferred_element_type=jnp.float32,
     )
-    for copy in reversed(late):
-        copy.wait()
-    total += near_in[...]
-    for mask in range(2, n_hours):
-        total += far_in[mask - 2].astype(jnp.float32)
+    bit = 1
+    while bit < n_hours:
+        copies[bit].wait()
+        arrived = near_in if bit == 1 else far_in
+        total += arrived[bit - 1].astype(jnp.float32)
+        bit *= 2
     local = total
     local_out[...] = local
 
     me = users * n_hours + hours
-    folded, diagonal = pack(dot_nt(local, local, HIGHEST))
+    folded, diagonal = pack(square(local))
     grams[me, pl.ds(0, k // 4), :] = folded
     grams[me, pl.ds(k // 4, 1), :] = diagonal
+    pl.semaphore_wait(row_ready, n_users - 1)
     copies = []
     for index, peer in enumerate(peers):
         copy = pltpu.make_async_remote_copy(
@@ -340,7 +379,6 @@
     k = sketch.shape[1]
     share = rows // n_hours
     dma = lambda count: pltpu.SemaphoreType.DMA((count,))
-    one = pltpu.SemaphoreType.DMA
     vmem = pl.BlockSpec(memory_space=pltpu.VMEM)
     local, gram = pl.pallas_call(
         functools.partial(kernel, n_users, n_hours),
@@ -357,16 +395,16 @@
             pltpu.VMEM((k, width), jnp.bfloat16),
             pltpu.VMEM((TAPS * k + PICK, width), jnp.bfloat16),
             pltpu.VMEM((TAPS, rows), jnp.float32),
-            pltpu.VMEM((k, share), jnp.float32),
-            pltpu.VMEM((k, share), jnp.float32),
-            pltpu.VMEM((n_hours - 2, k, share), jnp.bfloat16),
-            pltpu.VMEM((n_hours - 2, k, share), jnp.bfloat16),
-            pltpu.VMEM((n_hours - 1, SEAM, share), jnp.float32),
-            pltpu.VMEM((n_hours, SEAM, share), jnp.float32),
-            pltpu.VMEM((n_hours, k, EDGE), jnp.float32),
+            pltpu.VMEM((n_hours - 1, k, share), jnp.float32),
+            pltpu.VMEM((n_hours - 1, k, share), jnp.float32),
+            pltpu.VMEM((n_hours - 1, k, share), jnp.bfloat16),
+            pltpu.VMEM((n_hours - 1, k, share), jnp.bfloat16),
+            pltpu.VMEM((n_hours - 1, 2 * SEAM, share // 2), jnp.bfloat16),
+            pltpu.VMEM((n_hours, 2 * SEAM, share // 2), jnp.bfloat16),
+            pltpu.VMEM((n_hours, SEAM, EDGE), jnp.float32),
             pltpu.VMEM((n_users * n_hours, k // 4 + 1, 2 * k), jnp.float32),
-            dma(2 * n_hours), dma(3), one, one,
-            dma(n_hours - 2), dma(n_hours - 2), dma(n_hours - 1), dma(n_hours - 1),
+            pltpu.SemaphoreType.REGULAR, dma(2 * n_hours), dma(3),
+            dma(n_hours - 1), dma(n_hours - 1), dma(n_hours - 1), dma(n_hours - 1),
             dma(n_hours - 1), dma(n_hours - 1),
             dma(n_users * n_hours - 1), dma(n_users * n_hours - 1),
         ],

time: 22.3 us -> 20.2 us (0.906)
  Pallas kernels: 21.5 us -> 19.4 us
    pallas_call x1, Pallas kernels: 18.8 us -> 17 us  [per_device(): pl.pallas_call(functools.partial(kernel, n_users, n_hours), out_shape=(pl...]
    pallas_call x1, Pallas kernels: 2.73 us -> 2.34 us  [per_device(): pl.pallas_call(functools.partial(finish, 1.0 / math.sqrt(rows * n_users))...]
where the time goes in v4:
time: 20.2 us; the launch traced here: 20 us
  Pallas kernels  19.4 us (96%)
  between operations  0.64 us (3%)
    pallas_call x1, Pallas kernels, per_device(): pl.pallas_call(functools.partial(kernel, n_users, n_hours), out_shape=(pl...  17 us
    pallas_call x1, Pallas kernels, per_device(): pl.pallas_call(functools.partial(finish, 1.0 / math.sqrt(rows * n_users))...  2.34 us

profile of v4, /device:TPU:0, one launch (start us, length us, event | category | flops | bytes accessed | tf_op | source)
XLA Modules:
  0.0 20.0 jit_solution(2875456856564733171)
XLA Ops:
  0.6 17.0 %range_finder.1 = (f32[64,512]{1,0:T(8,128)S(1)}, f32[17,128]{1,0:T(8,128)S(1)}) custom-call(bf16[2048,2048]{1,0:T(8,128)(2,1)} %activity.1, s32[1,2048]{1,0:T(1,128)} %bitcast.4, f32[16,9]{1,0:T(8,128)} %table_in.1, bf16[64,2048]{1,0:T(8,128)(2,1)} %bitcast.3), custom_call_target="tpu_custom_call" | custom-call | tf_op jit(solution)/shard_map/range_finder/pallas_call | solution.py:383
  17.6 2.3 %factor.1 = (f32[64,512]{1,0:T(8,128)}, f32[64,64]{1,0:T(8,128)}) custom-call(f32[64,512]{1,0:T(8,128)S(1)} %get-tuple-element.6.local, f32[17,128]{1,0:T(8,128)S(1)} %get-tuple-element.7.gram), custom_call_target="tpu_custom_call" | custom-call | tf_op jit(solution)/shard_map/factor/pallas_call | solution.py:419

commit v5 on v4

--- a/solution.py
+++ b/solution.py
@@ -73,8 +73,10 @@
 def square(values):
     main = values.astype(jnp.bfloat16)
     minor = (values - main.astype(jnp.float32)).astype(jnp.bfloat16)
-    both = dot_nt(main, minor)
-    return dot_nt(main, main) + (both + both.T)
+    return dot_nt(
+        jnp.concatenate([main, main, minor], axis=1),
+        jnp.concatenate([main, minor, main], axis=1),
+    )
 
 
 def pack(gram):
@@ -160,12 +162,6 @@
     fetch(0)
 
     barrier = pltpu.get_barrier_semaphore()
-    peers = [
-        {"users": flip(users, far), "hours": flip(hours, mask)}
-        for far in range(n_users - 1, -1, -1)
-        for mask in range(n_hours - 1, -1, -1)
-        if far or mask
-    ]
     columns = [{"users": flip(users, far)} for far in range(n_users - 1, 0, -1)]
     for peer in [{"hours": flip(hours, mask)} for mask in range(n_hours - 1, 0, -1)] + columns:
         pl.semaphore_signal(barrier, inc=1, device_id=peer, device_id_type=MESH)
@@ -336,25 +332,45 @@
     grams[me, pl.ds(0, k // 4), :] = folded
     grams[me, pl.ds(k // 4, 1), :] = diagonal
     pl.semaphore_wait(row_ready, n_users - 1)
-    copies = []
-    for index, peer in enumerate(peers):
-        copy = pltpu.make_async_remote_copy(
-            src_ref=grams.at[me],
-            dst_ref=grams.at[me],
-            send_sem=gram_send.at[index],
-            recv_sem=gram_recv.at[index],
-            device_id=peer,
-            device_id_type=MESH,
-        )
-        copy.start()
-        copies.append(copy)
-    for copy in copies:
+    upper_half = users // (n_users // 2)
+    outgoing, incoming = [], []
+    for index in range(n_users):
+        down = n_users - 2 - index
+        down += (down - users + n_users) // n_users
+        up = index + (index - users + n_users) // n_users
+        target = upper_half * up + (1 - upper_half) * down if index < n_users - 1 else users
+        for mask in range(n_hours - 1, -1, -1):
+            if index == n_users - 1 and mask == 0:
+                continue
+            beside = flip(hours, mask)
+            slot = target * n_hours + beside
+            copy = pltpu.make_async_remote_copy(
+                src_ref=grams.at[me],
+                dst_ref=grams.at[me],
+                send_sem=gram_send.at[slot],
+                recv_sem=gram_recv.at[me],
+                device_id={"users": target, "hours": beside},
+                device_id_type=MESH,
+            )
+            copy.start()
+            outgoing.append(copy)
+            incoming.append(
+                pltpu.make_async_remote_copy(
+                    src_ref=grams.at[slot],
+                    dst_ref=grams.at[slot],
+                    send_sem=gram_send.at[slot],
+                    recv_sem=gram_recv.at[slot],
+                    device_id={"users": target, "hours": beside},
+                    device_id_type=MESH,
+                )
+            )
+    for copy in incoming:
         copy.wait_recv()
     gram = grams[0]
     for slot in range(1, n_users * n_hours):
         gram = gram + grams[slot]
     gram_out[...] = gram
-    for copy in copies:
+    for copy in outgoing:
         copy.wait_send()
 
 
@@ -406,7 +422,7 @@
             pltpu.SemaphoreType.REGULAR, dma(2 * n_hours), dma(3),
             dma(n_hours - 1), dma(n_hours - 1), dma(n_hours - 1), dma(n_hours - 1),
             dma(n_hours - 1), dma(n_hours - 1),
-            dma(n_users * n_hours - 1), dma(n_users * n_hours - 1),
+            dma(n_users * n_hours), dma(n_users * n_hours),
         ],
         compiler_params=pltpu.CompilerParams(
             collective_id=0, has_side_effects=True, vmem_limit_bytes=48 * 1024 * 1024

time: 20.2 us -> 19.9 us (0.985)
  Pallas kernels: 19.4 us -> 19.1 us
    pallas_call x1, Pallas kernels: 17 us -> 16.8 us  [per_device(): pl.pallas_call(functools.partial(kernel, n_users, n_hours), out_shape=(pl...]
where the time goes in v5:
time: 19.9 us; the launch traced here: 19.7 us
  Pallas kernels  19.1 us (96%)
  between operations  0.64 us (3%)
    pallas_call x1, Pallas kernels, per_device(): pl.pallas_call(functools.partial(kernel, n_users, n_hours), out_shape=(pl...  16.8 us
    pallas_call x1, Pallas kernels, per_device(): pl.pallas_call(functools.partial(finish, 1.0 / math.sqrt(rows * n_users))...  2.34 us

profile of v5, /device:TPU:0, one launch (start us, length us, event | category | flops | bytes accessed | tf_op | source)
XLA Modules:
  0.0 19.7 jit_solution(13731307256193892537)
XLA Ops:
  0.6 16.8 %range_finder.1 = (f32[64,512]{1,0:T(8,128)S(1)}, f32[17,128]{1,0:T(8,128)S(1)}) custom-call(bf16[2048,2048]{1,0:T(8,128)(2,1)} %activity.1, s32[1,2048]{1,0:T(1,128)} %bitcast.4, f32[16,9]{1,0:T(8,128)} %table_in.1, bf16[64,2048]{1,0:T(8,128)(2,1)} %bitcast.3), custom_call_target="tpu_custom_call" | custom-call | tf_op jit(solution)/shard_map/range_finder/pallas_call | solution.py:399
  17.4 2.3 %factor.1 = (f32[64,512]{1,0:T(8,128)}, f32[64,64]{1,0:T(8,128)}) custom-call(f32[64,512]{1,0:T(8,128)S(1)} %get-tuple-element.6.local, f32[17,128]{1,0:T(8,128)S(1)} %get-tuple-element.7.gram), custom_call_target="tpu_custom_call" | custom-call | tf_op jit(solution)/shard_map/factor/pallas_call | solution.py:435

commit v6 on v5

--- a/solution.py
+++ b/solution.py
@@ -246,19 +246,12 @@
         picked = jnp.concatenate(picked, axis=0).astype(jnp.bfloat16)
         if mask == order[0]:
             pl.semaphore_wait(barrier, n_hours + n_users - 2)
-            for peer in columns:
-                pl.semaphore_signal(row_ready, inc=1, device_id=peer, device_id_type=MESH)
-            for other in range(1, n_hours):
-                small.append(send(
-                    rims.at[hours], rims.at[hours], rim_send.at[other - 1],
-                    rim_recv.at[other - 1], other,
-                ))
         if mask == 0:
             picks[hours] = picked
             continue
         bit = 1
         while mask + bit < n_hours and bit < mask & -mask:
-            copies[mask + bit].wait()
+            copies[mask + bit].wait_recv()
             arrived = near_in if bit == 1 else far_in
             total += arrived[mask + bit - 1].astype(jnp.float32)
             bit *= 2
@@ -269,6 +262,14 @@
             source.at[mask - 1], target.at[mask - 1], part_send.at[mask - 1],
             part_recv.at[mask - 1], mask & -mask,
         )
+        if mask == order[0]:
+            for peer in columns:
+                pl.semaphore_signal(row_ready, inc=1, device_id=peer, device_id_type=MESH)
+            for other in range(1, n_hours):
+                small.append(send(
+                    rims.at[hours], rims.at[hours], rim_send.at[other - 1],
+                    rim_recv.at[other - 1], other,
+                ))
         pick_out[mask - 1] = picked
         small.append(send(
             pick_out.at[mask - 1], picks.at[hours], pick_send.at[mask - 1],
@@ -276,7 +277,7 @@
         ))
 
     for copy in small:
-        copy.wait()
+        copy.wait_recv()
 
     depth = EDGE // REACH
     rest = depth - SEAM * (n_hours - 1)
@@ -320,7 +321,7 @@
     )
     bit = 1
     while bit < n_hours:
-        copies[bit].wait()
+        copies[bit].wait_recv()
         arrived = near_in if bit == 1 else far_in
         total += arrived[bit - 1].astype(jnp.float32)
         bit *= 2
@@ -364,6 +365,8 @@
                     device_id_type=MESH,
                 )
             )
+    for copy in small + list(copies.values()):
+        copy.wait_send()
     for copy in incoming:
         copy.wait_recv()
     gram = grams[0]

time: 19.9 us -> 19.9 us (level)
  no operation moved by 1% of the time
where the time goes in v6:
time: 19.9 us; the launch traced here: 19.7 us
  Pallas kernels  19.1 us (96%)
  between operations  0.64 us (3%)
    pallas_call x1, Pallas kernels, per_device(): pl.pallas_call(functools.partial(kernel, n_users, n_hours), out_shape=(pl...  16.7 us
    pallas_call x1, Pallas kernels, per_device(): pl.pallas_call(functools.partial(finish, 1.0 / math.sqrt(rows * n_users))...  2.34 us

profile of v6, /device:TPU:0, one launch (start us, length us, event | category | flops | bytes accessed | tf_op | source)
XLA Modules:
  0.0 19.7 jit_solution(8085866384632713136)
XLA Ops:
  0.6 16.7 %range_finder.1 = (f32[64,512]{1,0:T(8,128)S(1)}, f32[17,128]{1,0:T(8,128)S(1)}) custom-call(bf16[2048,2048]{1,0:T(8,128)(2,1)} %activity.1, s32[1,2048]{1,0:T(1,128)} %bitcast.4, f32[16,9]{1,0:T(8,128)} %table_in.1, bf16[64,2048]{1,0:T(8,128)(2,1)} %bitcast.3), custom_call_target="tpu_custom_call" | custom-call | tf_op jit(solution)/shard_map/range_finder/pallas_call | solution.py:402
  17.4 2.3 %factor.1 = (f32[64,512]{1,0:T(8,128)}, f32[64,64]{1,0:T(8,128)}) custom-call(f32[64,512]{1,0:T(8,128)S(1)} %get-tuple-element.6.local, f32[17,128]{1,0:T(8,128)S(1)} %get-tuple-element.7.gram), custom_call_target="tpu_custom_call" | custom-call | tf_op jit(solution)/shard_map/factor/pallas_call | solution.py:438

commit v7 on v5

--- a/solution.py
+++ b/solution.py
@@ -339,7 +339,7 @@
         down += (down - users + n_users) // n_users
         up = index + (index - users + n_users) // n_users
         target = upper_half * up + (1 - upper_half) * down if index < n_users - 1 else users
-        for mask in range(n_hours - 1, -1, -1):
+        for mask in [code ^ 1 for code in range(n_hours - 1, -1, -1)]:
             if index == n_users - 1 and mask == 0:
                 continue
             beside = flip(hours, mask)

time: 19.9 us -> 19.8 us (level)
  no operation moved by 1% of the time
where the time goes in v7:
time: 19.8 us; the launch traced here: 19.6 us
  Pallas kernels  19 us (96%)
  between operations  0.64 us (3%)
    pallas_call x1, Pallas kernels, per_device(): pl.pallas_call(functools.partial(kernel, n_users, n_hours), out_shape=(pl...  16.7 us
    pallas_call x1, Pallas kernels, per_device(): pl.pallas_call(functools.partial(finish, 1.0 / math.sqrt(rows * n_users))...  2.34 us

profile of v7, /device:TPU:0, one launch (start us, length us, event | category | flops | bytes accessed | tf_op | source)
XLA Modules:
  0.0 19.6 jit_solution(1757581882063229123)
XLA Ops:
  0.6 16.7 %range_finder.1 = (f32[64,512]{1,0:T(8,128)S(1)}, f32[17,128]{1,0:T(8,128)S(1)}) custom-call(bf16[2048,2048]{1,0:T(8,128)(2,1)} %activity.1, s32[1,2048]{1,0:T(1,128)} %bitcast.4, f32[16,9]{1,0:T(8,128)} %table_in.1, bf16[64,2048]{1,0:T(8,128)(2,1)} %bitcast.3), custom_call_target="tpu_custom_call" | custom-call | tf_op jit(solution)/shard_map/range_finder/pallas_call | solution.py:399
  17.3 2.3 %factor.1 = (f32[64,512]{1,0:T(8,128)}, f32[64,64]{1,0:T(8,128)}) custom-call(f32[64,512]{1,0:T(8,128)S(1)} %get-tuple-element.6.local, f32[17,128]{1,0:T(8,128)S(1)} %get-tuple-element.7.gram), custom_call_target="tpu_custom_call" | custom-call | tf_op jit(solution)/shard_map/factor/pallas_call | solution.py:435

commit v8 on v6

--- a/solution.py
+++ b/solution.py
@@ -340,7 +340,7 @@
         down += (down - users + n_users) // n_users
         up = index + (index - users + n_users) // n_users
         target = upper_half * up + (1 - upper_half) * down if index < n_users - 1 else users
-        for mask in range(n_hours - 1, -1, -1):
+        for mask in [code ^ 1 for code in range(n_hours - 1, -1, -1)]:
             if index == n_users - 1 and mask == 0:
                 continue
             beside = flip(hours, mask)

time: 19.9 us -> 19.8 us (level)
  no operation moved by 1% of the time
where the time goes in v8:
time: 19.8 us; the launch traced here: 19.6 us
  Pallas kernels  19 us (96%)
  between operations  0.64 us (3%)
    pallas_call x1, Pallas kernels, per_device(): pl.pallas_call(functools.partial(kernel, n_users, n_hours), out_shape=(pl...  16.6 us
    pallas_call x1, Pallas kernels, per_device(): pl.pallas_call(functools.partial(finish, 1.0 / math.sqrt(rows * n_users))...  2.34 us

profile of v8, /device:TPU:0, one launch (start us, length us, event | category | flops | bytes accessed | tf_op | source)
XLA Modules:
  0.0 19.6 jit_solution(12357921769076701561)
XLA Ops:
  0.6 16.6 %range_finder.1 = (f32[64,512]{1,0:T(8,128)S(1)}, f32[17,128]{1,0:T(8,128)S(1)}) custom-call(bf16[2048,2048]{1,0:T(8,128)(2,1)} %activity.1, s32[1,2048]{1,0:T(1,128)} %bitcast.4, f32[16,9]{1,0:T(8,128)} %table_in.1, bf16[64,2048]{1,0:T(8,128)(2,1)} %bitcast.3), custom_call_target="tpu_custom_call" | custom-call | tf_op jit(solution)/shard_map/range_finder/pallas_call | solution.py:402
  17.3 2.3 %factor.1 = (f32[64,512]{1,0:T(8,128)}, f32[64,64]{1,0:T(8,128)}) custom-call(f32[64,512]{1,0:T(8,128)S(1)} %get-tuple-element.6.local, f32[17,128]{1,0:T(8,128)S(1)} %get-tuple-element.7.gram), custom_call_target="tpu_custom_call" | custom-call | tf_op jit(solution)/shard_map/factor/pallas_call | solution.py:438
